TPU v7x, 256 devices: a whole 4x4x8 slice. The times are simulated.
256 devices in a mesh: sample: 64 (over x, z, core), tensor: 4 (over y).
Axes of the slice: x: 4, y: 4, z: 8, core: 2. Of those that a mesh axis runs over, the one named last changes fastest.
Arguments:
- queries: bfloat16 [64, 256, 8192], P('sample', None, 'tensor'), may hold values from -48 to 48
- resp_keys: bfloat16 [64, 256, 1024], P('sample', None, 'tensor'), may hold values from -6 to 6
- resp_values: bfloat16 [64, 256, 1024], P('sample', None, 'tensor'), may hold values from -6 to 6
- prompt_keys: bfloat16 [64, 1024, 1024], P('sample', 'tensor'), may hold values from -8 to 8
- prompt_values: bfloat16 [64, 1024, 1024], P('sample', 'tensor'), may hold values from -6 to 6
- out_grad: bfloat16 [64, 256, 8192], P('sample', None, 'tensor'), may hold values from -48 to 48
- lengths: int32 [64], P('sample'), may hold values from 64 to 256, as said below
- owner: int32 [1], replicated, may hold values from 0 to 63
Outputs:
- grad_queries: bfloat16 [64, 256, 8192], P('sample', None, 'tensor')
- grad_resp_keys: bfloat16 [64, 256, 1024], P('sample', None, 'tensor')
- grad_resp_values: bfloat16 [64, 256, 1024], P('sample', None, 'tensor')
- grad_prompt_keys: float32 [1024, 1024], P('sample', 'tensor')
- grad_prompt_values: float32 [1024, 1024], P('sample', 'tensor')
Inputs may be any that keep to these rules, and one draw needn't show every extreme that they name: `lengths`: some response has all 256 tokens live.
All inputs are finite; a program needn't handle non-finite values.
Results may differ from a plain program's by a relative error of at most 0.012.
The roundings to bfloat16 on the way count: a program that leaves them out, or rounds other values in their place, can miss the bound.
Values may be sent and summed in bfloat16 or wider, within the bound.
No kernel may reach another device: no remote copies, remote signals or barrier semaphores. Data moves between devices by JAX's collectives and lax.ppermute only.
A program may use at most 128 MiB of HBM per device.

v0:
```python
import math

import jax
import jax.numpy as jnp
from jax import lax
from jax.sharding import PartitionSpec as P

HD = 128
GROUP = 8


masked_score = -1e30


def from_root(value, axis, root):
    mine = lax.axis_index(axis) == root
    return lax.psum(jnp.where(mine, value, jnp.zeros_like(value)), axis)


def per_device(
    queries, resp_keys, resp_values, prompt_keys, prompt_values, out_grad, lengths, owner
):
    owner_rank = owner[0]
    slot_key, slot_value = (
        from_root(prompt_keys[0], "sample", owner_rank),
        from_root(prompt_values[0], "sample", owner_rank),
    )
    prompt_key, prompt_value = (
        lax.all_to_all(slot_key, "tensor", split_axis=1, concat_axis=0, tiled=True),
        lax.all_to_all(slot_value, "tensor", split_axis=1, concat_axis=0, tiled=True),
    )
    rows_here = queries.shape[1]
    prompt_rows = prompt_key.shape[0]
    local_groups = resp_keys.shape[2] // HD
    feature_width = local_groups * HD
    factor = 1.0 / math.sqrt(HD)
    length_one = lengths[0]
    query_heads = queries[0].reshape(rows_here, local_groups, GROUP, HD)
    all_keys = jnp.concatenate([prompt_key, resp_keys[0]], 0).reshape(
        prompt_rows + rows_here, local_groups, HD
    )
    all_values = jnp.concatenate([prompt_value, resp_values[0]], 0).reshape(
        prompt_rows + rows_here, local_groups, HD
    )
    row_index = jnp.arange(rows_here, dtype=jnp.int32)
    valid_rows = row_index < length_one
    masked_grad = jnp.where(valid_rows[:, None], out_grad[0], jnp.zeros_like(out_grad[0]))
    grad_heads = masked_grad.reshape(rows_here, local_groups, GROUP, HD)
    col_index = jnp.arange(prompt_rows + rows_here, dtype=jnp.int32)[None, :]
    own_index = col_index - prompt_rows
    allowed = (col_index < prompt_rows) | (own_index <= row_index[:, None]) & (
        own_index < length_one
    )
    scores = (
        jnp.einsum("rkgd,ckd->kgrc", query_heads, all_keys, preferred_element_type=jnp.float32)
        * factor
    )
    scores = jnp.where(allowed, scores, masked_score)
    top_score = jnp.max(scores, axis=-1, keepdims=True)
    totals = jnp.sum(jnp.exp(scores - top_score), axis=-1, keepdims=True)
    attn_probs = jnp.exp(scores - top_score) / totals
    probs_half = attn_probs.astype(jnp.bfloat16)
    attended = jnp.einsum(
        "kgrc,ckd->rkgd", probs_half, all_values, preferred_element_type=jnp.float32
    )
    row_dots = jnp.sum(grad_heads.astype(jnp.float32) * attended, axis=-1).transpose(1, 2, 0)
    grad_probs = jnp.einsum(
        "rkgd,ckd->kgrc", grad_heads, all_values, preferred_element_type=jnp.float32
    )
    grad_scores = attn_probs * (grad_probs - row_dots[..., None])
    scores_half = grad_scores.astype(jnp.bfloat16)
    grad_query = (
        jnp.einsum("kgrc,ckd->rkgd", scores_half, all_keys, preferred_element_type=jnp.float32)
        * factor
    )
    grad_query = grad_query.reshape(1, rows_here, -1).astype(jnp.bfloat16)
    key_own = (
        jnp.einsum(
            "kgrc,rkgd->ckd",
            scores_half[..., prompt_rows:],
            query_heads,
            preferred_element_type=jnp.float32,
        )
        * factor
    )
    value_own = jnp.einsum(
        "kgrc,rkgd->ckd",
        probs_half[..., prompt_rows:],
        grad_heads,
        preferred_element_type=jnp.float32,
    )
    key_own = key_own.reshape(1, rows_here, feature_width).astype(jnp.bfloat16)
    value_own = value_own.reshape(1, rows_here, feature_width).astype(jnp.bfloat16)
    key_prompt = (
        jnp.einsum(
            "kgrc,rkgd->ckd",
            scores_half[..., :prompt_rows],
            query_heads,
            preferred_element_type=jnp.float32,
        )
        * factor
    )
    value_prompt = jnp.einsum(
        "kgrc,rkgd->ckd",
        probs_half[..., :prompt_rows],
        grad_heads,
        preferred_element_type=jnp.float32,
    )
    grad_prompt_key, grad_prompt_value = (
        lax.psum_scatter(
            key_prompt.reshape(prompt_rows, feature_width),
            "sample",
            scatter_dimension=0,
            tiled=True,
        ),
        lax.psum_scatter(
            value_prompt.reshape(prompt_rows, feature_width),
            "sample",
            scatter_dimension=0,
            tiled=True,
        ),
    )
    return (grad_query, key_own, value_own, grad_prompt_key, grad_prompt_value)


def solution(mesh):
    placed = (
        P("sample", None, "tensor"),
        P("sample", None, "tensor"),
        P("sample", None, "tensor"),
        P("sample", "tensor", None),
        P("sample", "tensor", None),
        P("sample", None, "tensor"),
        P("sample"),
        P(),
    )
    return jax.shard_map(
        per_device,
        mesh=mesh,
        in_specs=placed,
        out_specs=(
            P("sample", None, "tensor"),
            P("sample", None, "tensor"),
            P("sample", None, "tensor"),
            P("sample", "tensor"),
            P("sample", "tensor"),
        ),
        check_vma=False,
    )
```

profile of v0, /device:TPU:8, one launch (start us, length us, event | category | flops | bytes accessed | tf_op | source)
XLA Modules:
  0.0 558.2 jit_solution(11505073107272987419)
XLA Ops:
  7.2 0.0 copy-start.2
  7.2 0.0 all-reduce.3.cloned.1.call-start
  8.0 0.1 broadcast_select_fusion.4
  8.0 0.4 all_to_all.27
  8.4 0.9 copy.36
  9.3 0.4 all_to_all.24
  9.7 0.9 copy.31
  10.5 0.0 all-reduce.3.cloned.1.call-update
  10.6 190.1 %all-reduce.3.cloned.1.call-done = (bf16[256,4,256]{2,0,1:T(8,128)(2,1)}, bf16[256,4,256]{2,0,1:T(8,128)(2,1)}) async-done(((bf16[256,4,256]{2,0,1:T(8,128)(2,1)}, bf16[256,4,256]{2,0,1:T(8,128)(2,1)}), (bf16[256,4,256]{2,0,1:T(8,128)(2,1)}, bf16[256,4,256]{2,0,1:T(8,128)(2,1)})) %all-reduce.3.cloned.1.call-update) | async-done | bytes 1048592 | tf_op jit(solution)/shard_map/psum | solution.py:17
  200.7 4.8 all-to-all-start
  206.2 1.0 copy.32
  207.2 0.1 copy.34
  207.3 1.0 copy.37
  208.3 0.1 copy.39
  208.4 2.3 copy.76
  210.7 0.0 copy-done.2
  210.7 1.3 copy.40
  212.1 0.1 all-to-all-done
  212.1 4.9 all-to-all-start.1
  217.0 0.0 reduce-scatter.3.cloned.1.call-start
  217.1 1.0 fusion.26
  218.1 0.1 concatenate.16
  218.2 0.1 copy.33
  218.3 5.4 all-to-all-done.1
  223.7 0.1 concatenate.19
  223.8 0.1 copy.38
  223.9 0.0 copy-start.5
  223.9 12.3 %fusion.57 = (f32[2,8,256]{2,1,0:T(8,128)S(1)}, f32[2,8,256,1280]{2,3,1,0:T(8,128)}) fusion(pred[256,1280]{0,1:T(8,128)(4,1)S(1)} %fusion.26, bf16[256,2,8,128]{0,3,2,1:T(8,128)(2,1)} %bitcast.100, bf16[256,2,128]{2,0,1:T(8,128)(2,1)S(1)} %copy.34, bf16[1024,2,128]{2,0,1:T(8,128)(2,1)S(1)} %copy.33), kind=kOutput, calls=%fused_computation.57 | convolution fusion | flops 1364460800 | bytes 23019520 | tf_op jit(solution)/shard_map/sub | solution.py:61
  236.2 0.0 copy-start.3
  236.2 8.4 %fusion.7 = bf16[2,8,256,1280]{2,3,1,0:T(8,128)(2,1)S(1)} fusion(f32[2,8,256,1280]{2,3,1,0:T(8,128)} %get-tuple-element.18, f32[2,8,256]{2,1,0:T(8,128)S(1)} %get-tuple-element.17), kind=kLoop, calls=%fused_computation.11 | loop fusion | flops 10485760 | bytes 31473664 | tf_op jit(solution)/shard_map/convert_element_type | solution.py:62
  244.6 0.0 copy-start
  244.7 0.0 copy-done.5
  244.7 3.9 copy-done
  248.6 0.0 copy-done.3
  248.6 1.6 fusion.18
  250.2 9.3 %fusion.2 = bf16[2,8,256,1280]{2,3,1,0:T(8,128)(2,1)S(1)} fusion(f32[2,8,256]{2,1,0:T(8,128)S(1)} %bitcast.109, f32[2,8,256,1280]{2,3,1,0:T(8,128)} %get-tuple-element.18, f32[2,8,256]{2,1,0:T(8,128)S(1)} %get-tuple-element.17, bf16[256,2,8,128]{0,3,2,1:T(8,128)(2,1)} %bitcast.96, pred[256]{0:T(512)(128)(4,1)S(1)} %iota_compare_fusion.2, ...), kind=kOutput, calls=%fused_computation.3 | convolution fusion | flops 1364983808 | bytes 33194240 | tf_op jit(solution)/shard_map/rkgd,ckd->kgrc/dot_general | solution.py:67
  259.5 0.0 copy-start.1
  259.5 4.0 copy-done.1
  263.5 5.0 fusion.22
  268.5 2.5 copy.51
  271.0 0.0 reduce-scatter.3.cloned.1.call-update
  271.0 0.2 reduce-scatter.5.cloned.1.call-start
  271.3 6.5 %fusion.8 = f32[2,128,1024,1]{2,1,3,0:T(8,128)S(1)} fusion(bf16[2,8,256,1280]{2,3,1,0:T(8,128)(2,1)} %copy-done, bf16[256,2,8,128]{0,3,2,1:T(8,128)(2,1)} %bitcast.97, pred[256]{0:T(512)(128)(4,1)S(1)} %iota_compare_fusion.2), kind=kOutput, calls=%fused_computation.12 | convolution fusion | flops 1074266112 | bytes 10486016 | tf_op jit(solution)/shard_map/kgrc,rkgd->ckd/dot_general | solution.py:103
  277.8 0.0 copy-start.4
  277.8 1.3 copy.53
  279.2 0.0 reduce-scatter.5.cloned.1.call-update
  279.2 5.7 %multiply_convert_fusion = bf16[2,128,8,256]{3,1,2,0:T(8,128)(2,1)S(1)} fusion(bf16[2,8,256,1280]{2,3,1,0:T(8,128)(2,1)} %copy-done.1, bf16[256,2,128]{2,0,1:T(8,128)(2,1)S(1)} %copy.34, bf16[1024,2,128]{2,0,1:T(8,128)(2,1)S(1)} %copy.33), kind=kOutput, calls=%fused_computation.23 | convolution fusion | flops 1344536576 | bytes 12189696 | tf_op jit(solution)/shard_map/kgrc,ckd->rkgd/dot_general | solution.py:73
  284.9 1.4 copy.54
  286.3 2.7 fusion.39
  289.0 0.8 copy.55
  289.7 0.0 copy-done.4
  289.7 2.4 fusion.36
  292.2 0.8 copy.56
  292.9 115.9 %reduce-scatter.3.cloned.1.call-done = f32[16,256]{1,0:T(8,128)} async-done(((f32[1024,256]{1,0:T(8,128)}), f32[16,256]{1,0:T(8,128)}) %reduce-scatter.3.cloned.1.call-update) | async-done | bytes 16400 | tf_op jit(solution)/shard_map/reduce_scatter | solution.py:110
  408.8 142.9 %reduce-scatter.5.cloned.1.call-done = f32[16,256]{1,0:T(8,128)} async-done(((f32[1024,256]{1,0:T(8,128)}), f32[16,256]{1,0:T(8,128)}) %reduce-scatter.5.cloned.1.call-update) | async-done | bytes 16400 | tf_op jit(solution)/shard_map/reduce_scatter | solution.py:116
  (3 shorter events, 0.0 us)
Async XLA Ops:
  7.2 203.6 %copy-start.2 = (bf16[1,256,2048]{2,1,0:T(8,128)(2,1)S(1)}, bf16[1,256,2048]{2,1,0:T(8,128)(2,1)}, u32[]{:S(2)}) copy-start(bf16[1,256,2048]{2,1,0:T(8,128)(2,1)} %param.13) | copy-start | bytes 3145732
  7.2 193.5 %all-reduce.3.cloned.1.call-start = ((), (), s32[]{:S(2)}) async-start(), calls=%async_computation.6 | async-start | bytes 2097152 | tf_op jit(solution)/shard_map/psum | solution.py:17
  200.7 11.4 %all-to-all-start = ((bf16[256,4,256]{2,0,1:T(8,128)(2,1)}), bf16[256,4,256]{2,0,1:T(8,128)(2,1)S(1)}, u32[]{:S(2)}, u32[]{:S(2)}) async-start(bf16[256,4,256]{2,0,1:T(8,128)(2,1)} %get-tuple-element.15), calls=%async_computation | async-start | bytes 1048576 | tf_op jit(solution)/shard_map/all_to_all | solution.py:29
  212.1 11.5 %all-to-all-start.1 = ((bf16[256,4,256]{2,0,1:T(8,128)(2,1)}), bf16[256,4,256]{2,0,1:T(8,128)(2,1)S(1)}, u32[]{:S(2)}, u32[]{:S(2)}) async-start(bf16[256,4,256]{2,0,1:T(8,128)(2,1)} %get-tuple-element.16), calls=%async_computation.1 | async-start | bytes 1048576 | tf_op jit(solution)/shard_map/all_to_all | solution.py:30
  217.0 191.7 %reduce-scatter.3.cloned.1.call-start = ((), (), s32[]{:S(2)}) async-start(), calls=%async_computation.4 | async-start | bytes 1064960 | tf_op jit(solution)/shard_map/reduce_scatter | solution.py:110
  223.9 20.8 %copy-start.5 = (bf16[1024,2,128]{2,0,1:T(8,128)(2,1)}, bf16[1024,2,128]{2,0,1:T(8,128)(2,1)S(1)}, u32[]{:S(2)}) copy-start(bf16[1024,2,128]{2,0,1:T(8,128)(2,1)S(1)} %copy.38) | copy-start | bytes 1572868
  236.2 12.4 %copy-start.3 = (bf16[1,256,2048]{1,2,0:T(8,128)(2,1)S(1)}, bf16[1,256,2048]{1,2,0:T(8,128)(2,1)}, u32[]{:S(2)}) copy-start(bf16[1,256,2048]{1,2,0:T(8,128)(2,1)} %copy.40) | copy-start | bytes 3145732
  244.6 4.0 copy-start
  259.5 4.0 copy-start.1
  271.0 280.6 %reduce-scatter.5.cloned.1.call-start = ((), (), s32[]{:S(2)}) async-start(), calls=%async_computation.5 | async-start | bytes 1064960 | tf_op jit(solution)/shard_map/reduce_scatter | solution.py:116
  277.8 11.9 %copy-start.4 = (bf16[1,256,2048]{1,2,0:T(8,128)(2,1)S(1)}, bf16[1,256,2048]{1,2,0:T(8,128)(2,1)}, u32[]{:S(2)}) copy-start(bf16[1,256,2048]{1,2,0:T(8,128)(2,1)} %copy.40) | copy-start | bytes 3145732
Sparse Core Ops, SparseCore 0:
  12.1 188.5 all-reduce.2
  271.2 137.5 reduce-scatter.2
  413.9 137.7 reduce-scatter.4
where the time goes:
time: 559 us; the launch traced here: 558 us
  waiting for transfers between devices  454 us (81%)
  matrix products  45.5 us (8%)
  local copies, waits for them, and re-layouts  23.5 us (4%)
  between operations  15.3 us (3%)
  starting transfers between devices  9.98 us (2%)
  other arithmetic  9.56 us (2%)
    psum x1, waiting for transfers between devices, from_root(): return lax.psum(jnp.where(mine, value, jnp.zeros_like(value)), axis)  190 us
    reduce_scatter x1, waiting for transfers between devices, per_device(): lax.psum_scatter(value_prompt.reshape(prompt_rows, feature_width), 'sampl...  143 us
    reduce_scatter x1, waiting for transfers between devices, per_device(): lax.psum_scatter(key_prompt.reshape(prompt_rows, feature_width), 'sample'...  116 us
    unnamed x18, local copies, waits for them, and re-layouts  14.2 us
    sub x1, matrix products, per_device(): attn_probs = jnp.exp(scores - top_score) / totals  12.3 us
  transfers between devices with their start and end apart: 5, of which 5 were waited for; matrix products, arithmetic and copies ran while one was open for 5% of the time, Pallas kernels for 0%

commit v1 on v0

v1 whole, which is shorter than its diff:
```python
import math

import jax
import jax.numpy as jnp
from jax import lax
from jax.experimental import pallas as pl
from jax.experimental.pallas import tpu as pltpu
from jax.sharding import Mesh
from jax.sharding import PartitionSpec as P

HD = 128
GROUP = 8
HEADS_PER_STEP = 4
X, Z, CORES = 4, 8, 2
CHIPS = X * Z
FACTOR = 1.0 / math.sqrt(HD)
TO_EXP2 = FACTOR * math.log2(math.e)
masked_score = -1e30
f32, bf16 = jnp.float32, jnp.bfloat16
CHIP_AXES = ("x", "z")
SWAP = [(0, 1), (1, 0)]


def dot(a, b, over=((1,), (0,))):
    return lax.dot_general(a, b, (over, ((), ())), preferred_element_type=f32)


def attention_kernel(
    flags, q_ref, g_ref, mine_ref, other_ref, ko_ref, vo_ref, *rest
):
    dq_ref, dko_ref, dvo_ref, keep_ref, send_ref = rest[-11:-6]
    k_all, v_all, k_turned, acc_k, acc_v, _ = rest[-6:]
    step, last = pl.program_id(0), pl.num_programs(0) - 1
    length, core = flags[0], flags[1]
    prompt, own, rows = mine_ref.shape[0], ko_ref.shape[0], q_ref.shape[0]

    @pl.when(step == 0)
    def _():
        @pl.when(core == 0)
        def _():
            k_all[:prompt] = mine_ref[...]
            v_all[:prompt] = other_ref[...]

        @pl.when(core != 0)
        def _():
            k_all[:prompt] = other_ref[...]
            v_all[:prompt] = mine_ref[...]

        k_all[prompt:] = ko_ref[...]
        v_all[prompt:] = vo_ref[...]
        k_turned[...] = k_all[...].T
        acc_k[...] = jnp.zeros_like(acc_k)
        acc_v[...] = jnp.zeros_like(acc_v)

    live = lax.broadcasted_iota(jnp.int32, (rows, 1), 0) < length
    key = lax.broadcasted_iota(jnp.int32, (own, rows), 0)
    row = lax.broadcasted_iota(jnp.int32, (own, rows), 1)
    allowed = (key <= row) & (key < length)
    turned = ((1,), (1,))
    for head in range(HEADS_PER_STEP):
        cols = slice(head * HD, (head + 1) * HD)
        q = q_ref[:, cols]
        g = jnp.where(live, g_ref[:, cols], 0).astype(bf16)
        s_p = dot(k_all[:prompt], q, turned)
        s_o = jnp.where(allowed, dot(k_all[prompt:], q, turned), masked_score)
        top = jnp.maximum(
            jnp.max(s_p, 0, keepdims=True), jnp.max(s_o, 0, keepdims=True)
        )
        e_p = jnp.exp2((s_p - top) * TO_EXP2)
        e_o = jnp.exp2((s_o - top) * TO_EXP2)
        total = jnp.sum(e_p, 0, keepdims=True) + jnp.sum(e_o, 0, keepdims=True)
        inverse = 1.0 / total
        p_p, p_o = e_p * inverse, e_o * inverse
        h_p, h_o = p_p.astype(bf16), p_o.astype(bf16)
        g_p = dot(v_all[:prompt], g, turned)
        g_o = dot(v_all[prompt:], g, turned)
        row_dot = jnp.sum(h_p.astype(f32) * g_p, 0, keepdims=True) + jnp.sum(
            h_o.astype(f32) * g_o, 0, keepdims=True
        )
        d_p = (p_p * (g_p - row_dot)).astype(bf16)
        d_o = (p_o * (g_o - row_dot)).astype(bf16)
        acc_v[:prompt] += dot(h_p, g)
        acc_v[prompt:] += dot(h_o, g)
        acc_k[:prompt] += dot(d_p, q)
        acc_k[prompt:] += dot(d_o, q)
        dq = dot(k_turned[:, :prompt], d_p) + dot(k_turned[:, prompt:], d_o)
        dq_ref[:, cols] = (dq.T * FACTOR).astype(bf16)

    @pl.when(step == last)
    def _():
        acc_k[...] = acc_k[...] * FACTOR
        dko_ref[...] = acc_k[prompt:].astype(bf16)
        dvo_ref[...] = acc_v[prompt:].astype(bf16)
        for chip in range(CHIPS):
            for which, acc in enumerate((acc_k, acc_v)):
                for half in range(2):
                    start = ((chip % 8) * 4 + half) * 32 + (chip // 8) * 8
                    to = slice(half * 8, half * 8 + 8)
                    keep_at = pl.multiple_of(start + core * 64, 8)
                    send_at = pl.multiple_of(start + (1 - core) * 64, 8)
                    keep_ref[chip, which, to] = acc[pl.ds(keep_at, 8)]
                    rest[-1][which, to] = acc[pl.ds(send_at, 8)]
                send_ref[chip, which] = rest[-1][which].astype(bf16)


def attention(flags, q, g, mine, other, ko, vo, group, carried):
    rows, prompt, own = q.shape[0], mine.shape[0], ko.shape[0]
    steps = GROUP // HEADS_PER_STEP
    heads = pl.BlockSpec((rows, HEADS_PER_STEP * HD), lambda s, f: (0, group * steps + s))
    whole = pl.BlockSpec((prompt, HD), lambda s, f: (0, 0))
    part = pl.BlockSpec((own, HD), lambda s, f: (0, group))
    share = pl.BlockSpec((CHIPS, 2, 16, HD), lambda s, f: (0, 0, 0, 0))
    keys = prompt + own
    return pl.pallas_call(
        attention_kernel,
        grid_spec=pltpu.PrefetchScalarGridSpec(
            num_scalar_prefetch=1,
            grid=(steps,),
            in_specs=[heads, heads, whole, whole, part, part]
            + [pl.BlockSpec(memory_space=pl.ANY)] * len(carried),
            out_specs=[heads, part, part, share, share],
            scratch_shapes=[
                pltpu.VMEM((keys, HD), bf16),
                pltpu.VMEM((keys, HD), bf16),
                pltpu.VMEM((HD, keys), bf16),
                pltpu.VMEM((keys, HD), f32),
                pltpu.VMEM((keys, HD), f32),
                pltpu.VMEM((2, 16, HD), f32),
            ],
        ),
        out_shape=[
            jax.ShapeDtypeStruct(q.shape, bf16),
            jax.ShapeDtypeStruct(ko.shape, bf16),
            jax.ShapeDtypeStruct(vo.shape, bf16),
            jax.ShapeDtypeStruct((CHIPS, 2, 16, HD), f32),
            jax.ShapeDtypeStruct((CHIPS, 2, 16, HD), bf16),
        ],
        input_output_aliases={7 + i: i for i in range(len(carried))},
        compiler_params=pltpu.CompilerParams(vmem_limit_bytes=48 * 1024 * 1024),
        cost_estimate=pl.CostEstimate(
            flops=12 * GROUP * rows * keys * HD,
            bytes_accessed=4 * 1024 * 1024,
            transcendentals=GROUP * rows * keys,
        ),
        name=f"attention_{group}",
    )(flags, q, g, mine, other, ko, vo, *carried)


def per_device(
    queries, resp_keys, resp_values, prompt_keys, prompt_values, out_grad, lengths, owner
):
    core = lax.axis_index("core")
    owner_chip, owner_core = owner[0] // CORES, owner[0] % CORES
    groups = resp_keys.shape[2] // HD
    tensors = lax.axis_size("tensor")
    block = prompt_keys.shape[1]
    piece = block // CHIPS

    pk, pv = prompt_keys[0], prompt_values[0]
    got = lax.ppermute(jnp.where(core == 0, pv, pk), "core", SWAP)
    slot = jnp.where(core == owner_core, jnp.where(core == 0, pk, pv), got)
    slot = slot.reshape(CHIPS, piece, tensors, groups, HD)

    flags = jnp.stack([lengths[0], core.astype(jnp.int32)])
    rows = []
    for group in range(groups):
        out = slot[:, :, :, group].transpose(0, 2, 1, 3)
        out = out.reshape(CHIPS * tensors, piece, HD)
        arrived = lax.all_to_all(out, ("x", "z", "tensor"), 0, 0, tiled=True)
        picked = lax.dynamic_slice_in_dim(arrived, owner_chip * tensors, tensors, 0)
        picked = picked.reshape(1, tensors * piece, HD)
        out = jnp.broadcast_to(picked, (CHIPS, tensors * piece, HD))
        mine = lax.all_to_all(out, CHIP_AXES, 0, 0, tiled=True)
        mine = mine.reshape(CHIPS * tensors * piece, HD)
        rows.append((mine, lax.ppermute(mine, "core", SWAP)))

    carried, sums = (), []
    for group in range(groups):
        mine, other = rows[group]
        *carried, keep, send = attention(
            flags, queries[0], out_grad[0], mine, other, resp_keys[0], resp_values[0], group, carried
        )
        pair = keep + lax.ppermute(send, "core", SWAP).astype(f32)
        shares = lax.all_to_all(pair.astype(bf16), CHIP_AXES, 0, 0, tiled=True)
        sums.append(jnp.sum(shares.astype(f32), axis=0))
    dq, dko, dvo = carried
    return (
        dq[None],
        dko[None],
        dvo[None],
        jnp.concatenate([s[0] for s in sums], axis=1),
        jnp.concatenate([s[1] for s in sums], axis=1),
    )


def solution(mesh):
    split = Mesh(
        mesh.devices.reshape(X, Z, CORES, mesh.shape["tensor"]),
        ("x", "z", "core", "tensor"),
    )
    sample = ("x", "z", "core")
    placed = (
        P(sample, None, "tensor"),
        P(sample, None, "tensor"),
        P(sample, None, "tensor"),
        P(sample, "tensor", None),
        P(sample, "tensor", None),
        P(sample, None, "tensor"),
        P(sample),
        P(),
    )
    return jax.shard_map(
        per_device,
        mesh=split,
        in_specs=placed,
        out_specs=(
            P(sample, None, "tensor"),
            P(sample, None, "tensor"),
            P(sample, None, "tensor"),
            P(sample, "tensor"),
            P(sample, "tensor"),
        ),
        check_vma=False,
    )
```

time: 559 us -> 151 us (0.27)
  waiting for transfers between devices: 454 us -> 59 us
  matrix products: 45.5 us -> 0 us
  blocking collectives: 0 us -> 29.4 us
  Pallas kernels: 0 us -> 27.4 us
  local copies, waits for them, and re-layouts: 23.5 us -> 2.32 us
  starting transfers between devices: 9.98 us -> 25.8 us
  between operations: 15.3 us -> 2.15 us
  other arithmetic: 9.56 us -> 3.58 us
    reduce_scatter x2 -> x0, waiting for transfers between devices: 259 us -> none  [the longest x1 143 us: per_device(): lax.psum_scatter(value_prompt.reshape(prompt_rows, feature_width), 'sampl...]
    psum x1 -> x0, waiting for transfers between devices: 190 us -> none  [from_root(): return lax.psum(jnp.where(mine, value, jnp.zeros_like(value)), axis)]
    all_to_all x2 -> x5, waiting for transfers between devices: 5.43 us -> 57.8 us  [the longest x2 23.6 us: per_device(): shares = lax.all_to_all(pair.astype(bf16), CHIP_AXES, 0, 0, tiled=True)]
    dot_general x7 -> x0, matrix products: 33.2 us -> none  [the longest x1 9.26 us: per_device(): jnp.einsum('rkgd,ckd->kgrc', grad_heads, all_values, preferred_element_ty...]
    all_to_all x0 -> x1, blocking collectives: none -> 29.4 us  [per_device(): arrived = lax.all_to_all(out, ('x', 'z', 'tensor'), 0, 0, tiled=True)]
    pallas_call x0 -> x2, Pallas kernels: none -> 27.4 us  [attention(): pl.pallas_call(attention_kernel, grid_spec=pltpu.PrefetchScalarGridSpec(n...]
    all_to_all x2 -> x5, starting transfers between devices: 9.72 us -> 25.1 us  [the longest x2 9.63 us: per_device(): shares = lax.all_to_all(pair.astype(bf16), CHIP_AXES, 0, 0, tiled=True)]
    unnamed x18 -> x12, local copies, waits for them, and re-layouts: 14.2 us -> 0.02 us
  transfers between devices with their start and end apart: 5 -> 10, of which waited for: 5 -> 6; matrix products, arithmetic and copies ran while one was open for 5% -> 1% of each run, Pallas kernels for 0% -> 18%
where the time goes in v1:
time: 151 us; the launch traced here: 150 us
  waiting for transfers between devices  59 us (39%)
  blocking collectives  29.4 us (19%)
  Pallas kernels  27.4 us (18%)
  starting transfers between devices  25.8 us (17%)
  other arithmetic  3.58 us (2%)
  local copies, waits for them, and re-layouts  2.32 us (2%)
  between operations  2.15 us (1%)
    all_to_all x1, blocking collectives, per_device(): arrived = lax.all_to_all(out, ('x', 'z', 'tensor'), 0, 0, tiled=True)  29.4 us
    pallas_call x2, Pallas kernels, attention(): pl.pallas_call(attention_kernel, grid_spec=pltpu.PrefetchScalarGridSpec(n...  27.4 us
    all_to_all x2, waiting for transfers between devices, per_device(): shares = lax.all_to_all(pair.astype(bf16), CHIP_AXES, 0, 0, tiled=True)  23.6 us
    all_to_all x2, waiting for transfers between devices, per_device(): mine = lax.all_to_all(out, CHIP_AXES, 0, 0, tiled=True)  21.1 us
    all_to_all x1, waiting for transfers between devices, per_device(): arrived = lax.all_to_all(out, ('x', 'z', 'tensor'), 0, 0, tiled=True)  13 us
    all_to_all x2, starting transfers between devices, per_device(): shares = lax.all_to_all(pair.astype(bf16), CHIP_AXES, 0, 0, tiled=True)  9.63 us
    all_to_all x2, starting transfers between devices, per_device(): mine = lax.all_to_all(out, CHIP_AXES, 0, 0, tiled=True)  8.37 us
    all_to_all x1, starting transfers between devices, per_device(): arrived = lax.all_to_all(out, ('x', 'z', 'tensor'), 0, 0, tiled=True)  7.13 us
  transfers between devices with their start and end apart: 10, of which 6 were waited for; matrix products, arithmetic and copies ran while one was open for 1% of the time, Pallas kernels for 18%

profile of v1, /device:TPU:8, one launch (start us, length us, event | category | flops | bytes accessed | tf_op | source)
XLA Modules:
  0.0 149.6 jit_solution(11113275965419152629)
XLA Ops:
  0.6 0.0 copy-start.4
  0.6 0.0 copy-start.5
  0.7 1.2 select_bitcast_fusion
  1.9 0.1 collective-permute-start
  2.6 1.2 collective-permute-done
  3.9 0.0 copy-done.4
  3.9 0.0 copy-done.5
  3.9 0.1 bitcast_select_fusion
  3.9 0.8 fusion
  4.7 0.0 copy-start.2
  4.7 0.0 copy-start.3
  4.7 29.4 %all_to_all.30 = bf16[128,8,128]{2,1,0:T(8,128)(2,1)S(1)} all-to-all(bf16[128,8,128]{2,1,0:T(8,128)(2,1)S(1)} %bitcast.55), channel_id=1, replica_groups=mesh['x'=4,'z'=8,'core'=2,'tensor'=4] {'x','z','tensor'}, dimensions={0} | all-to-all | bytes 524288 | tf_op jit(solution)/shard_map/all_to_all | solution.py:169
  34.1 0.0 copy-start
  34.1 0.0 copy-start.1
  34.1 7.1 %all-to-all-start = ((bf16[128,8,128]{2,1,0:T(8,128)(2,1)}), bf16[128,8,128]{2,1,0:T(8,128)(2,1)S(1)}, u32[]{:S(2)}, u32[]{:S(2)}) async-start(bf16[128,8,128]{2,1,0:T(8,128)(2,1)} %bitcast.9), calls=%async_computation | async-start | bytes 524288 | tf_op jit(solution)/shard_map/all_to_all | solution.py:169
  41.3 13.0 %all-to-all-done = bf16[128,8,128]{2,1,0:T(8,128)(2,1)S(1)} async-done(((bf16[128,8,128]{2,1,0:T(8,128)(2,1)}), bf16[128,8,128]{2,1,0:T(8,128)(2,1)S(1)}, u32[]{:S(2)}, u32[]{:S(2)}) %all-to-all-start) | async-done | bytes 262176 | tf_op jit(solution)/shard_map/all_to_all | solution.py:169
  54.3 0.7 broadcast_in_dim.26
  55.0 3.9 %all-to-all-start.3 = ((bf16[32,32,128]{2,1,0:T(8,128)(2,1)}), bf16[32,32,128]{2,1,0:T(8,128)(2,1)S(1)}, u32[]{:S(2)}, u32[]{:S(2)}) async-start(bf16[32,32,128]{2,1,0:T(8,128)(2,1)} %broadcast_in_dim.26), calls=%async_computation.3 | async-start | bytes 524288 | tf_op jit(solution)/shard_map/all_to_all | solution.py:173
  58.9 10.9 %all-to-all-done.3 = bf16[32,32,128]{2,1,0:T(8,128)(2,1)S(1)} async-done(((bf16[32,32,128]{2,1,0:T(8,128)(2,1)}), bf16[32,32,128]{2,1,0:T(8,128)(2,1)S(1)}, u32[]{:S(2)}, u32[]{:S(2)}) %all-to-all-start.3) | async-done | bytes 262176 | tf_op jit(solution)/shard_map/all_to_all | solution.py:173
  69.9 0.7 broadcast_in_dim.24
  70.6 4.5 %all-to-all-start.1 = ((bf16[32,32,128]{2,1,0:T(8,128)(2,1)}), bf16[32,32,128]{2,1,0:T(8,128)(2,1)S(1)}, u32[]{:S(2)}, u32[]{:S(2)}) async-start(bf16[32,32,128]{2,1,0:T(8,128)(2,1)} %broadcast_in_dim.24), calls=%async_computation.1 | async-start | bytes 524288 | tf_op jit(solution)/shard_map/all_to_all | solution.py:173
  75.1 0.1 collective-permute-start.2
  75.9 0.1 pad_add_fusion.flags
  75.9 10.2 %all-to-all-done.1 = bf16[32,32,128]{2,1,0:T(8,128)(2,1)S(1)} async-done(((bf16[32,32,128]{2,1,0:T(8,128)(2,1)}), bf16[32,32,128]{2,1,0:T(8,128)(2,1)S(1)}, u32[]{:S(2)}, u32[]{:S(2)}) %all-to-all-start.1) | async-done | bytes 262176 | tf_op jit(solution)/shard_map/all_to_all | solution.py:173
  86.1 0.0 collective-permute-start.1
  86.1 0.0 collective-permute-done.2.other_ref
  86.1 0.0 copy-done.2
  86.1 0.0 copy-done.3
  86.1 0.0 copy-done
  86.1 0.0 copy-done.1
  86.1 13.7 %attention_0.1 = (bf16[256,2048]{1,0:T(8,128)(2,1)}, bf16[256,256]{1,0:T(8,128)(2,1)}, bf16[256,256]{1,0:T(8,128)(2,1)}, f32[32,2,16,128]{3,2,1,0:T(8,128)S(1)}, bf16[32,2,16,128]{3,2,1,0:T(8,128)(2,1)S(1)}) custom-call(s32[2]{0:T(128)S(1)} %pad_add_fusion.flags, bf16[256,2048]{1,0:T(8,128)(2,1)S(1)} %bitcast.46, bf16[256,2048]{1,0:T(8,128)(2,1)S(1)} %bitcast.48, ...), custom_call_target="tpu_custom_call" | custom-call | flops 4026531840 | bytes 4194304 | tf_op jit(solution)/shard_map/attention_0/pallas_call | solution.py:114
  99.8 0.5 collective-permute-start.3
  100.3 0.0 collective-permute-done.1.other_ref
  100.3 13.7 %attention_1.1 = (bf16[256,2048]{1,0:T(8,128)(2,1)}, bf16[256,256]{1,0:T(8,128)(2,1)}, bf16[256,256]{1,0:T(8,128)(2,1)}, f32[32,2,16,128]{3,2,1,0:T(8,128)S(1)}, bf16[32,2,16,128]{3,2,1,0:T(8,128)(2,1)S(1)}) custom-call(s32[2]{0:T(128)S(1)} %pad_add_fusion.flags, ...), custom_call_target="tpu_custom_call", output_to_operand_aliasing={{0}: (7, {}), {1}: (8, {}), {2}: (9, {})} | custom-call | flops 4026531840 | bytes 4194304 | tf_op jit(solution)/shard_map/attention_1/pallas_call | solution.py:114
  114.0 0.0 collective-permute-start.4
  114.0 0.0 collective-permute-done.3
  114.0 0.8 add_convert_fusion.1
  114.8 4.5 %all-to-all-start.4 = ((bf16[32,2,16,128]{3,2,1,0:T(8,128)(2,1)}), bf16[32,2,16,128]{3,2,1,0:T(8,128)(2,1)S(1)}, u32[]{:S(2)}, u32[]{:S(2)}) async-start(bf16[32,2,16,128]{3,2,1,0:T(8,128)(2,1)} %add_convert_fusion.1), calls=%async_computation.4 | async-start | bytes 524288 | tf_op jit(solution)/shard_map/all_to_all | solution.py:184
  119.3 0.0 collective-permute-done.4
  119.3 0.8 add_convert_fusion
  120.1 11.6 %all-to-all-done.4 = bf16[32,2,16,128]{3,2,1,0:T(8,128)(2,1)S(1)} async-done(((bf16[32,2,16,128]{3,2,1,0:T(8,128)(2,1)}), bf16[32,2,16,128]{3,2,1,0:T(8,128)(2,1)S(1)}, u32[]{:S(2)}, u32[]{:S(2)}) %all-to-all-start.4) | async-done | bytes 262176 | tf_op jit(solution)/shard_map/all_to_all | solution.py:184
  131.7 5.1 %all-to-all-start.5 = ((bf16[32,2,16,128]{3,2,1,0:T(8,128)(2,1)}), bf16[32,2,16,128]{3,2,1,0:T(8,128)(2,1)S(1)}, u32[]{:S(2)}, u32[]{:S(2)}) async-start(bf16[32,2,16,128]{3,2,1,0:T(8,128)(2,1)} %add_convert_fusion), calls=%async_computation.5 | async-start | bytes 524288 | tf_op jit(solution)/shard_map/all_to_all | solution.py:184
  136.9 12.1 %all-to-all-done.5 = bf16[32,2,16,128]{3,2,1,0:T(8,128)(2,1)S(1)} async-done(((bf16[32,2,16,128]{3,2,1,0:T(8,128)(2,1)}), bf16[32,2,16,128]{3,2,1,0:T(8,128)(2,1)S(1)}, u32[]{:S(2)}, u32[]{:S(2)}) %all-to-all-start.5) | async-done | bytes 262176 | tf_op jit(solution)/shard_map/all_to_all | solution.py:184
  149.0 0.6 pad_maximum_fusion
  (6 shorter events, 0.1 us)
Async XLA Ops:
  0.6 3.2 %copy-start.4 = (bf16[1,256,1024]{2,1,0:T(8,128)(2,1)S(1)}, bf16[1,256,1024]{2,1,0:T(8,128)(2,1)}, u32[]{:S(2)}) copy-start(bf16[1,256,1024]{2,1,0:T(8,128)(2,1)} %param.12) | copy-start | bytes 1572868
  0.6 3.2 %copy-start.5 = (bf16[1,256,1024]{2,1,0:T(8,128)(2,1)S(1)}, bf16[1,256,1024]{2,1,0:T(8,128)(2,1)}, u32[]{:S(2)}) copy-start(bf16[1,256,1024]{2,1,0:T(8,128)(2,1)} %param.11) | copy-start | bytes 1572868
  1.9 2.0 %collective-permute-start = (bf16[256,1024]{1,0:T(8,128)(2,1)S(1)}, bf16[256,1024]{1,0:T(8,128)(2,1)S(1)}, u32[]{:S(2)}, u32[]{:S(2)}) collective-permute-start(bf16[256,1024]{1,0:T(8,128)(2,1)S(1)} %select_bitcast_fusion), channel_id=1, source_target_pairs={{0,4},{4,0},{1,5},{5,1},{2,6},{6,2},{3,7},{7,3},{8,12},{12,8},{9,1... | collective-permute-start | bytes 1572872 | tf_op jit(solution)/shard_map/ppermute | solution.py:160
  4.7 81.4 %copy-start.2 = (bf16[1,256,256]{2,1,0:T(8,128)(2,1)S(1)}, bf16[1,256,256]{2,1,0:T(8,128)(2,1)}, u32[]{:S(2)}) copy-start(bf16[1,256,256]{2,1,0:T(8,128)(2,1)} %param.9) | copy-start | bytes 393220
  4.7 81.4 %copy-start.3 = (bf16[1,256,256]{2,1,0:T(8,128)(2,1)S(1)}, bf16[1,256,256]{2,1,0:T(8,128)(2,1)}, u32[]{:S(2)}) copy-start(bf16[1,256,256]{2,1,0:T(8,128)(2,1)} %param.10) | copy-start | bytes 393220
  34.1 52.0 %copy-start = (bf16[1,256,2048]{2,1,0:T(8,128)(2,1)S(1)}, bf16[1,256,2048]{2,1,0:T(8,128)(2,1)}, u32[]{:S(2)}) copy-start(bf16[1,256,2048]{2,1,0:T(8,128)(2,1)} %param.8) | copy-start | bytes 3145732
  34.1 52.0 %copy-start.1 = (bf16[1,256,2048]{2,1,0:T(8,128)(2,1)S(1)}, bf16[1,256,2048]{2,1,0:T(8,128)(2,1)}, u32[]{:S(2)}) copy-start(bf16[1,256,2048]{2,1,0:T(8,128)(2,1)} %param.13) | copy-start | bytes 3145732
  34.1 20.2 %all-to-all-start = ((bf16[128,8,128]{2,1,0:T(8,128)(2,1)}), bf16[128,8,128]{2,1,0:T(8,128)(2,1)S(1)}, u32[]{:S(2)}, u32[]{:S(2)}) async-start(bf16[128,8,128]{2,1,0:T(8,128)(2,1)} %bitcast.9), calls=%async_computation | async-start | bytes 524288 | tf_op jit(solution)/shard_map/all_to_all | solution.py:169
  55.0 14.8 %all-to-all-start.3 = ((bf16[32,32,128]{2,1,0:T(8,128)(2,1)}), bf16[32,32,128]{2,1,0:T(8,128)(2,1)S(1)}, u32[]{:S(2)}, u32[]{:S(2)}) async-start(bf16[32,32,128]{2,1,0:T(8,128)(2,1)} %broadcast_in_dim.26), calls=%async_computation.3 | async-start | bytes 524288 | tf_op jit(solution)/shard_map/all_to_all | solution.py:173
  70.6 15.5 %all-to-all-start.1 = ((bf16[32,32,128]{2,1,0:T(8,128)(2,1)}), bf16[32,32,128]{2,1,0:T(8,128)(2,1)S(1)}, u32[]{:S(2)}, u32[]{:S(2)}) async-start(bf16[32,32,128]{2,1,0:T(8,128)(2,1)} %broadcast_in_dim.24), calls=%async_computation.1 | async-start | bytes 524288 | tf_op jit(solution)/shard_map/all_to_all | solution.py:173
  75.1 11.0 %collective-permute-start.2 = (bf16[1024,128]{1,0:T(8,128)(2,1)S(1)}, bf16[1024,128]{1,0:T(8,128)(2,1)S(1)}, u32[]{:S(2)}, u32[]{:S(2)}) collective-permute-start(bf16[1024,128]{1,0:T(8,128)(2,1)S(1)} %bitcast.42), channel_id=1, source_target_pairs={{0,4},{4,0},{1,5},{5,1},{2,6},{6,2},{3,7},{7,3},{8,12},{12,8},{9,1... | collective-permute-start | bytes 786440 | tf_op jit(solution)/shard_map/ppermute | solution.py:175
  86.1 14.2 %collective-permute-start.1 = (bf16[1024,128]{1,0:T(8,128)(2,1)S(1)}, bf16[1024,128]{1,0:T(8,128)(2,1)S(1)}, u32[]{:S(2)}, u32[]{:S(2)}) collective-permute-start(bf16[1024,128]{1,0:T(8,128)(2,1)S(1)} %bitcast.44), channel_id=1, source_target_pairs={{0,4},{4,0},{1,5},{5,1},{2,6},{6,2},{3,7},{7,3},{8,12},{12,8},{9,1... | collective-permute-start | bytes 786440 | tf_op jit(solution)/shard_map/ppermute | solution.py:175
  99.8 14.2 %collective-permute-start.3 = (bf16[32,2,16,128]{3,2,1,0:T(8,128)(2,1)S(1)}, bf16[32,2,16,128]{3,2,1,0:T(8,128)(2,1)S(1)}, u32[]{:S(2)}, u32[]{:S(2)}) collective-permute-start(bf16[32,2,16,128]{3,2,1,0:T(8,128)(2,1)S(1)} %get-tuple-element.22), channel_id=1, source_target_pairs={{0,4},{4,0},{1,5},{5,1},{2,6},{6,2},{3,7},{7,3},{8,12},{12,8},{9,1... | collective-permute-start | bytes 786440 | tf_op jit(solution)/shard_map/ppermute | solution.py:183
  114.0 5.3 %collective-permute-start.4 = (bf16[32,2,16,128]{3,2,1,0:T(8,128)(2,1)S(1)}, bf16[32,2,16,128]{3,2,1,0:T(8,128)(2,1)S(1)}, u32[]{:S(2)}, u32[]{:S(2)}) collective-permute-start(bf16[32,2,16,128]{3,2,1,0:T(8,128)(2,1)S(1)} %get-tuple-element.24), channel_id=1, source_target_pairs={{0,4},{4,0},{1,5},{5,1},{2,6},{6,2},{3,7},{7,3},{8,12},{12,8},{9,1... | collective-permute-start | bytes 786440 | tf_op jit(solution)/shard_map/ppermute | solution.py:183
  114.8 16.9 %all-to-all-start.4 = ((bf16[32,2,16,128]{3,2,1,0:T(8,128)(2,1)}), bf16[32,2,16,128]{3,2,1,0:T(8,128)(2,1)S(1)}, u32[]{:S(2)}, u32[]{:S(2)}) async-start(bf16[32,2,16,128]{3,2,1,0:T(8,128)(2,1)} %add_convert_fusion.1), calls=%async_computation.4 | async-start | bytes 524288 | tf_op jit(solution)/shard_map/all_to_all | solution.py:184
  131.7 17.3 %all-to-all-start.5 = ((bf16[32,2,16,128]{3,2,1,0:T(8,128)(2,1)}), bf16[32,2,16,128]{3,2,1,0:T(8,128)(2,1)S(1)}, u32[]{:S(2)}, u32[]{:S(2)}) async-start(bf16[32,2,16,128]{3,2,1,0:T(8,128)(2,1)} %add_convert_fusion), calls=%async_computation.5 | async-start | bytes 524288 | tf_op jit(solution)/shard_map/all_to_all | solution.py:184
